TPU v7x, 32 devices: a whole 2x2x4 slice. The times are simulated.
32 devices in a mesh: member: 2 (over y), gx: 4 (over z), gy: 4 (over x, core).
Axes of the slice: x: 2, y: 2, z: 4, core: 2. Of those that a mesh axis runs over, the one named last changes fastest.
Arguments:
- checkpoint: float32 [8, 4, 4, 12288], P(('member', 'gx'), 'gy'), parts along dimension 0, may hold values from -6 to 6
- holder_list: int32 [8, 4, 4], P(('member', 'gx'), 'gy'), parts along dimension 0, may hold values from 0 to 3, each once within a row
- height: float32 [64, 512], P(('member', 'gx'), 'gy'), parts along dimension 0, may hold values from -6 to 6
- land_mask: int32 [32, 512], P('gx', 'gy'), may hold values 0 or 1
- diffusivity: float32 [3, 16], replicated, may hold values from 0.02 to 0.2
- tracer_weight: float32 [6, 16, 32, 512], P('member', None, 'gx', 'gy'), parts along dimension 0, may hold values from -6 to 6
- height_weight: float32 [64, 512], P(('member', 'gx'), 'gy'), parts along dimension 0, may hold values from -6 to 6
Outputs:
- adjoint_tracers: float32 [6, 16, 32, 512], P('member', None, 'gx', 'gy'), parts along dimension 0
- adjoint_height: float32 [64, 512], P(('member', 'gx'), 'gy'), parts along dimension 0
There are 2 independent parts, one for each index of `member`. A program takes and returns all parts, laid end to end along the dimension named above; an argument that names none is the same for every part. Nothing has to cross between parts.
Inputs may be any that keep to these rules, and one draw needn't show every extreme that they name: For each owner device (o, g), holder_list[o, g, :] names every longitude index once: each device along gx holds exactly one piece of every owner's tracers in its row.
All inputs are finite; a program needn't handle non-finite values. No bound on the sum of `land_mask` on one device may be relied on, other than what follows from the above.
Results may differ from a plain program's by a relative error of at most 0.0001.
Values sent between devices are 32-bit elements; how exact they have to be, the bound alone decides.
A program may use at most 64 MiB of HBM per device.

v0:
```python
import functools
import jax
import jax.numpy as jnp
from jax import lax
from jax.experimental import pallas as pl
from jax.experimental.pallas import tpu as pltpu
from jax.sharding import PartitionSpec as P

ITERS = 4
ADVECTION = 0.3
VERTICAL_MIX = 0.1
HEIGHT_DIFFUSION = 0.2
HEIGHT_DAMPING = 0.3
BUOYANCY = 0.5

SUB = 8
LANE = 128
HALO = 4
GROUP = 16
GROUPS = LANE // GROUP
MESH = pl.DeviceIdType.MESH


def roll_lanes(value, shift):
    return pltpu.roll(value, shift, 1)


def roll_rows(value, shift):
    return pltpu.roll(value, shift, 0)


def kernel(
    n, n_y, levels, piece_rows,
    holder_hbm, diff_hbm, ckpt_hbm, height_hbm, mask_hbm, tw_hbm, hw_hbm,
    out_ref, outh_ref,
    buf, recv, state, strip, lam, slam, mu, smu, dy, sdy, pairs, sdiff,
    hf, af, bf, wf, lh, gu, gv, prow,
    em, es, el, zq, zl, xs, xr, ys, yr,
    holder_ref, diff_ref, ckpt_ref, height_ref, mask_ref, hw_ref,
    a2a_send, a2a_recv, send_sem, recv_sem, in_sem,
):
    me = lax.axis_index("gx")
    my = lax.axis_index("gy")
    east, west = lax.rem(me + 1, n), lax.rem(me + n - 1, n)
    north, south = lax.rem(my + 1, n_y), lax.rem(my + n_y - 1, n_y)
    channels = 3 * levels
    each = channels // GROUPS
    padded = -(-piece_rows // SUB) * SUB
    own = slice(SUB, 2 * SUB)
    blocks = (HALO, HALO + SUB)

    inputs = (
        (ckpt_hbm, ckpt_ref), (diff_hbm, diff_ref), (mask_hbm, mask_ref), (tw_hbm, lam.at[:, pl.ds(SUB, SUB)]),
        (height_hbm, height_ref), (hw_hbm, hw_ref), (holder_hbm, holder_ref),
    )
    loads = [pltpu.make_async_copy(source, target, in_sem.at[i]) for i, (source, target) in enumerate(inputs)]
    for load in loads:
        load.start()

    barrier = pltpu.get_barrier_semaphore()
    for k in range(1, n):
        pl.semaphore_signal(barrier, inc=1, device_id={"gx": lax.rem(me + k, n)}, device_id_type=MESH)
    for other in (north, south):
        pl.semaphore_signal(barrier, inc=1, device_id={"gy": other}, device_id_type=MESH)
        for side in (east, west):
            pl.semaphore_signal(barrier, inc=1, device_id={"gx": side, "gy": other}, device_id_type=MESH)

    loads[0].wait()
    if padded != piece_rows:
        buf[...] = jnp.zeros_like(buf)
    for o in range(0, n, SUB):
        size = min(SUB, n - o)
        for r in range(piece_rows):
            buf[pl.ds(o * padded + r, size, stride=padded), :] = ckpt_ref[o:o + size, r * LANE:(r + 1) * LANE]

    pl.semaphore_wait(barrier, n + 5)

    mine = pl.multiple_of(me * padded, SUB)
    sends = []
    a2a = []
    for k in range(1, n):
        owner = lax.rem(me + k, n)
        copy = pltpu.make_async_remote_copy(
            src_ref=buf.at[pl.ds(pl.multiple_of(owner * padded, SUB), padded)],
            dst_ref=recv.at[me],
            send_sem=a2a_send.at[k], recv_sem=a2a_recv.at[k],
            device_id={"gx": owner}, device_id_type=MESH,
        )
        copy.start()
        a2a.append(copy)
    recv[me] = buf[pl.ds(mine, padded), :]

    used = [0]

    def send(source, target, device):
        i = used[0]
        used[0] += 1
        copy = pltpu.make_async_remote_copy(
            src_ref=source, dst_ref=target, send_sem=send_sem.at[i], recv_sem=recv_sem.at[i],
            device_id=device, device_id_type=MESH,
        )
        copy.start()
        sends.append(copy)
        return copy

    def wait_all(copies):
        for copy in copies:
            copy.wait_recv()

    lane = lax.broadcasted_iota(jnp.int32, (SUB, LANE), 1)
    sub = lax.broadcasted_iota(jnp.int32, (SUB, LANE), 0)
    first_lane, last_lane = lane == 0, lane == LANE - 1
    group = lax.shift_right_logical(lane, 4)
    place = lane & (GROUP - 1)
    low, high = place < HALO, place >= GROUP - HALO
    half = place < GROUP // 2
    edge = place == HALO - 1
    below, above = jnp.where(low, my, 1), jnp.where(high, n_y - 1 - my, 1)
    inside = (below > 0) & (above > 0)
    zero = jnp.zeros((SUB, LANE), jnp.float32)

    def back(value, shift):
        return roll_lanes(value, (LANE - shift) % LANE)

    def everywhere(value):
        moved = [value] + [roll_lanes(value, GROUP * k) for k in range(1, GROUPS)]
        while len(moved) > 1:
            moved = [a + b for a, b in zip(moved[::2], moved[1::2])]
        return moved[0]

    def edges(from_south, from_north):
        return jnp.where(edge, from_south, back(from_north, GROUP - 2 * HALO + 2))

    def side_of(pair, g):
        return back(pair, g * GROUP + HALO - 1)

    def channel_of(s):
        return group * each + s

    def first_level(s):
        return (channel_of(s) & (levels - 1)) == 0

    def last_level(s):
        return (channel_of(s) & (levels - 1)) == levels - 1

    def level_up(c):
        return c - lax.div(lax.rem(c, levels) + (levels - 1), levels)

    def level_down(c):
        return c + lax.div(2 * (levels - 1) - lax.rem(c, levels), levels)

    def over(body, carry=0):
        return lax.fori_loop(0, each, body, carry, unroll=2)

    def pack_field(value):
        south_part = (lane >= HALO) & (lane < 2 * HALO)
        north_part = (lane >= 2 * HALO) & (lane < 3 * HALO)
        picked = jnp.where(south_part, roll_lanes(value, HALO), jnp.where(north_part, roll_lanes(value, 3 * HALO), 0.0))
        return everywhere(picked)

    def pack_strip(ref, s, rows):
        packed = zero
        for g in range(GROUPS):
            moved = roll_lanes(ref[g * each + s, rows, :], (g * GROUP + 2 * HALO) % LANE)
            packed = jnp.where(group == g, moved, packed)
        return packed

    def send_strips(which, ref):
        def body(q, carry):
            a, b = pack_strip(ref, 2 * q, own), pack_strip(ref, 2 * q + 1, own)
            zq[which, q] = jnp.where(half, back(a, HALO), roll_lanes(b, HALO))
            return carry

        lax.fori_loop(0, each // 2, body, 0, unroll=True)
        whole = zq.at[which]
        copies = []
        for side, other in enumerate((north, south)):
            for start, device in (
                (SUB, {"gy": other}), (0, {"gx": east, "gy": other}), (2 * SUB, {"gx": west, "gy": other}),
            ):
                copies.append(send(whole, zl.at[which, side, :, pl.ds(start, SUB)], device))
        return copies

    def build_strips(which, ref, put):
        def body(q, carry):
            for g in blocks:
                rows = slice(g, g + SUB)
                south_pair, north_pair = zl[which, 0, q, rows, :], zl[which, 1, q, rows, :]
                for k, (from_south, from_north) in enumerate((
                    (south_pair, roll_lanes(north_pair, GROUP // 2)), (back(south_pair, GROUP // 2), north_pair),
                )):
                    packed = pack_strip(ref, 2 * q + k, rows)
                    mid = jnp.where(half, back(packed, HALO), roll_lanes(packed, HALO))
                    value = jnp.where(low, from_south, jnp.where(high, from_north, mid))
                    put(2 * q + k, rows, jnp.where(inside, value, 0.0))
            return carry

        lax.fori_loop(0, each // 2, body, 0)

    def send_rows(ref, out, into, width, to_east, to_west):
        count = channels * width // SUB
        place_of = lax.div(sub, width)
        for side, start in enumerate((to_east, to_west)):
            def body(k, carry):
                value = zero
                for j in range(SUB // width):
                    rows = slice(start - width * j, start - width * j + SUB)
                    value = jnp.where(place_of == j, ref[k + j * count, rows, :], value)
                out[side, k] = value
                return carry

            lax.fori_loop(0, count, body, 0, unroll=4)
        return [send(out.at[0], into.at[0], {"gx": east}), send(out.at[1], into.at[1], {"gx": west})]

    def take_rows(ref, into, width, from_west, from_east):
        count = channels * width // SUB

        def body(k, carry):
            for side, (base, offset) in enumerate(((0, from_west), (2 * SUB, from_east - 2 * SUB))):
                value = into[side, k]
                rows = slice(base, base + SUB)
                mask = (sub >= offset) & (sub < offset + width)
                for j in range(SUB // width):
                    shift = (offset - width * j) % SUB
                    c = k + j * count
                    ref[c, rows, :] = jnp.where(mask, roll_rows(value, shift) if shift else value, ref[c, rows, :])
            return carry

        lax.fori_loop(0, count, body, 0, unroll=4)

    def send_fields(first, values):
        for k, value in enumerate(values):
            em[first + k, own, :] = value
            es[first + k] = pack_field(value)
        which = pl.ds(first, len(values))
        mid, before, after = pl.ds(SUB, SUB), pl.ds(0, SUB), pl.ds(2 * SUB, SUB)
        copies = [
            send(em.at[which, mid], em.at[which, before], {"gx": east}),
            send(em.at[which, mid], em.at[which, after], {"gx": west}),
        ]
        for side, other in enumerate((north, south)):
            copies.append(send(es.at[which], el.at[side, which, mid], {"gy": other}))
            copies.append(send(es.at[which], el.at[side, which, before], {"gx": east, "gy": other}))
            copies.append(send(es.at[which], el.at[side, which, after], {"gx": west, "gy": other}))
        return copies

    def take_field(k, target):
        for r in range(0, 3 * SUB, SUB):
            rows = slice(r, r + SUB)
            value = em[k, rows, :]
            piece = jnp.where(
                low, back(el[0, k, rows, :], GROUP // 2),
                jnp.where(high, roll_lanes(el[1, k, rows, :], GROUP // 2), pack_field(value)),
            )
            target[0, rows, :] = value
            target[1, rows, :] = jnp.where(inside, piece, 0.0)

    def along(field, g, shift):
        return field[0, g + shift:g + shift + SUB, :], field[1, g + shift:g + shift + SUB, :]

    def latitude(main, piece):
        side = side_of(edges(piece, piece), 0)
        h_n = jnp.where(last_lane, side, back(main, 1))
        h_s = jnp.where(first_lane, side, roll_lanes(main, 1))
        return h_n, h_s, back(piece, 1), roll_lanes(piece, 1)

    def total_of(step, rows):
        main = state[step, 0, rows, :]
        for c in range(1, levels):
            main = main + state[step, c, rows, :]
        piece = zero
        for s in range(each):
            piece = piece + jnp.where(channel_of(s) < levels, strip[step, s + 1, rows, :], 0.0)
        return main, everywhere(piece)

    def slopes(step, advance):
        for g in blocks:
            rows = slice(g, g + SUB)
            main, piece = along(hf.at[step], g, 0)
            main_e, piece_e = along(hf.at[step], g, 1)
            main_w, piece_w = along(hf.at[step], g, -1)
            main_n, main_s, piece_n, piece_s = latitude(main, piece)
            af[step, 0, rows, :] = (-0.25 * ADVECTION) * (main_n - main_s)
            af[step, 1, rows, :] = (-0.25 * ADVECTION) * (piece_n - piece_s)
            bf[step, 0, rows, :] = (0.25 * ADVECTION) * (main_e - main_w)
            bf[step, 1, rows, :] = (0.25 * ADVECTION) * (piece_e - piece_w)
            if not advance:
                continue
            totals = total_of(step, rows)
            for k, (h, h_e, h_w, h_n, h_s) in enumerate((
                (main, main_e, main_w, main_n, main_s), (piece, piece_e, piece_w, piece_n, piece_s),
            )):
                lap = h_e + h_w + h_n + h_s - 4.0 * h
                value = h + HEIGHT_DIFFUSION * lap - HEIGHT_DAMPING * jnp.tanh(h)
                value = value + (BUOYANCY / levels) * wf[k, rows, :] * totals[k]
                hf[step + 1, k, rows, :] = jnp.where(inside, value, 0.0) if k else value

    def wrap_strips(ref):
        for g in blocks:
            rows = slice(g, g + SUB)
            ref[0, rows, :] = roll_lanes(ref[each, rows, :], GROUP)
            ref[each + 1, rows, :] = back(ref[1, rows, :], GROUP)

    def strip_vertical(ref, s, rows, value):
        upper = jnp.where(first_level(s), value, ref[s, rows, :])
        lower = jnp.where(last_level(s), value, ref[s + 2, rows, :])
        return upper + lower - 2.0 * value

    for load in loads[1:]:
        load.wait()
    fields_a = send_fields(0, (height_ref[...], mask_ref[...].astype(jnp.float32), hw_ref[...]))

    for s in range(each):
        value = zero
        for g in range(GROUPS):
            c = g * each + s
            value = jnp.where(group == g, diff_ref[c // levels, c % levels], value)
        sdiff[s] = value
    for step in range(1, ITERS):
        for k in range(2):
            hf[step, k, 0:SUB, :] = zero
            hf[step, k, 2 * SUB:3 * SUB, :] = zero
    for k in range(2):
        for r in range(0, 3 * SUB, SUB):
            gu[k, r:r + SUB, :] = zero
            gv[k, r:r + SUB, :] = zero

    for copy in a2a:
        copy.wait_recv()
    first = state.at[0]
    for p in range(n):
        holder = holder_ref[0, 0, p]
        if piece_rows % SUB == 0:
            depth = piece_rows // SUB
            for c in range(depth):
                first[p * depth + c, own, :] = recv[holder, c * SUB:(c + 1) * SUB, :]
        else:
            for r in range(piece_rows):
                row = p * piece_rows + r
                at = SUB + row % SUB
                first[row // SUB, at:at + 1, :] = recv[holder, r:r + 1, :]

    start_copies = send_rows(first, xs.at[0], xr.at[0], HALO, 3 * HALO, 2 * HALO)
    start_copies += send_strips(0, first)
    weight_copies = send_rows(lam, xs.at[1], xr.at[1], HALO, 3 * HALO, 2 * HALO)
    weight_copies += send_strips(1, lam)

    wait_all(fields_a)
    take_field(0, hf.at[0])
    take_field(1, wf)
    take_field(2, lh)

    def put_first(s, rows, value):
        strip[0, s + 1, rows, :] = value
        pairs[s, rows, :] = edges(value, value)

    wait_all(start_copies)
    take_rows(first, xr.at[0], HALO, HALO, 2 * SUB)
    build_strips(0, first, put_first)
    wrap_strips(strip.at[0])

    def forward(step):
        def body(s, carry):
            for r in blocks:
                rows, rows_e, rows_w = (slice(r + d, r + d + SUB) for d in (0, 1, -1))
                pair = pairs[s, rows, :]
                a, b, w = af[step, 0, rows, :], bf[step, 0, rows, :], wf[0, rows, :]
                for g in range(GROUPS):
                    c = g * each + s
                    value = state[step, c, rows, :]
                    side = side_of(pair, g)
                    c_s = jnp.where(first_lane, side, roll_lanes(value, 1))
                    c_n = jnp.where(last_lane, side, back(value, 1))
                    c_e, c_w = state[step, c, rows_e, :], state[step, c, rows_w, :]
                    vert = state[step, level_up(c), rows, :] + state[step, level_down(c), rows, :] - 2.0 * value
                    delta = c_n - c_s
                    if step < 2:
                        dy[step, c, rows, :] = delta
                    lap = c_e + c_w + c_n + c_s - 4.0 * value
                    d = diff_ref[lax.div(c, levels), lax.rem(c, levels)]
                    state[step + 1, c, rows, :] = value + w * (
                        d * lap - a * (c_e - c_w) - b * delta + VERTICAL_MIX * vert
                    )
                a, b, w = af[step, 1, rows, :], bf[step, 1, rows, :], wf[1, rows, :]
                value = strip[step, s + 1, rows, :]
                c_s, c_n = roll_lanes(value, 1), back(value, 1)
                c_e, c_w = strip[step, s + 1, rows_e, :], strip[step, s + 1, rows_w, :]
                delta = c_n - c_s
                if step < 2:
                    sdy[step, s, rows, :] = delta
                lap = c_e + c_w + c_n + c_s - 4.0 * value
                vert = strip_vertical(strip.at[step], s, rows, value)
                value = value + w * (sdiff[s] * lap - a * (c_e - c_w) - b * delta + VERTICAL_MIX * vert)
                strip[step + 1, s + 1, rows, :] = value
                pairs[s, rows, :] = edges(value, value)
            return carry

        over(body)

    outer_copies, fields_b = [], []
    for step in range(ITERS - 1):
        slopes(step, True)
        if step == 1:
            fields_b = send_fields(3, (hf[2, 0, own, :],))
        forward(step)
        if step == 1:
            outer_copies = send_rows(state.at[2], ys, yr, 2, 3 * HALO, 2 * HALO + 2)
            outer_copies += send_strips(2, state.at[2])
        if step < 2:
            wrap_strips(strip.at[step + 1])
    slopes(3, False)

    def last_sums(s, carry):
        total_u, total_v = carry
        pair = pairs[s, own, :]
        for g in range(GROUPS):
            c = g * each + s
            value = state[3, c, own, :]
            side = side_of(pair, g)
            m = wf[0, own, :] * lam[c, own, :]
            delta = jnp.where(last_lane, side, back(value, 1)) - jnp.where(first_lane, side, roll_lanes(value, 1))
            total_u = total_u + m * (state[3, c, SUB + 1:2 * SUB + 1, :] - state[3, c, SUB - 1:2 * SUB - 1, :])
            total_v = total_v + m * delta
        return total_u, total_v

    total_u, total_v = over(last_sums, (zero, zero))
    fields_c = send_fields(4, (total_u, total_v, hf[3, 0, own, :], af[3, 0, own, :]))

    def put_weight(s, rows, value):
        slam[s, rows, :] = value

    wait_all(weight_copies)
    take_rows(lam, xr.at[1], HALO, HALO, 2 * SUB)
    build_strips(1, lam, put_weight)

    def spread_pair(step, s, rows, m):
        bm = bf[step, 1, rows, :] * m
        dm = sdiff[s] * m
        pairs[s, rows, :] = edges(dm - bm, dm + bm)

    def put_outer(s, rows, value):
        sdy[2, s, rows, :] = back(value, 1) - roll_lanes(value, 1)
        strip[2, s + 1, rows, :] = value
        pairs[s, rows, :] = edges(value, value)

    wait_all(outer_copies)
    take_rows(state.at[2], yr, 2, HALO, 2 * SUB + 2)
    build_strips(2, state.at[2], put_outer)

    def outer_slopes(s, carry):
        for r in blocks:
            rows = slice(r, r + SUB)
            pair = pairs[s, rows, :]
            for g in range(GROUPS):
                c = g * each + s
                value = state[2, c, rows, :]
                side = side_of(pair, g)
                dy[2, c, rows, :] = (
                    jnp.where(last_lane, side, back(value, 1)) - jnp.where(first_lane, side, roll_lanes(value, 1))
                )
        return carry

    over(outer_slopes)
    wait_all(fields_b)
    take_field(3, hf.at[2])
    slopes(2, False)
    wait_all(fields_c)
    take_field(4, gu)
    take_field(5, gv)
    take_field(6, hf.at[3])
    slopes(3, False)
    take_field(7, af.at[3])
    for copy in a2a + sends:
        copy.wait_send()

    def weigh(s, carry):
        for r in blocks:
            rows = slice(r, r + SUB)
            for g in range(GROUPS):
                c = g * each + s
                mu[c, rows, :] = wf[0, rows, :] * lam[c, rows, :]
            m = wf[1, rows, :] * slam[s, rows, :]
            smu[s + 1, rows, :] = m
            spread_pair(3, s, rows, m)
        return carry

    def sums(step):
        def body(s, carry):
            result = []
            for r, (total_u, total_v, strip_u, strip_v) in zip(blocks, (carry[:4], carry[4:])):
                rows, rows_e, rows_w = (slice(r + d, r + d + SUB) for d in (0, 1, -1))
                w = wf[0, rows, :]
                for g in range(GROUPS):
                    c = g * each + s
                    m = w * lam[c, rows, :]
                    mu[c, rows, :] = m
                    total_u = total_u + m * (state[step, c, rows_e, :] - state[step, c, rows_w, :])
                    total_v = total_v + m * dy[step, c, rows, :]
                m = wf[1, rows, :] * slam[s, rows, :]
                smu[s + 1, rows, :] = m
                strip_u = strip_u + m * (strip[step, s + 1, rows_e, :] - strip[step, s + 1, rows_w, :])
                strip_v = strip_v + m * sdy[step, s, rows, :]
                spread_pair(step, s, rows, m)
                result += [total_u, total_v, strip_u, strip_v]
            return tuple(result)

        totals = over(body, (zero,) * 8)
        for r, (total_u, total_v, strip_u, strip_v) in zip(blocks, (totals[:4], totals[4:])):
            rows = slice(r, r + SUB)
            gu[0, rows, :], gv[0, rows, :] = total_u, total_v
            gu[1, rows, :], gv[1, rows, :] = everywhere(strip_u), everywhere(strip_v)

    def adjoint(step):
        last = step == 0

        def body(s, carry):
            for r in (SUB,) if last else blocks:
                rows, rows_e, rows_w = (slice(r + d, r + d + SUB) for d in (0, 1, -1))
                pair = pairs[s, rows, :]
                a_e, a_w, b = af[step, 0, rows_e, :], af[step, 0, rows_w, :], bf[step, 0, rows, :]
                push = prow[0, rows, :]
                for g in range(GROUPS):
                    c = g * each + s
                    m = mu[c, rows, :]
                    m_e, m_w = mu[c, rows_e, :], mu[c, rows_w, :]
                    vert = mu[level_up(c), rows, :] + mu[level_down(c), rows, :] - 2.0 * m
                    d = diff_ref[lax.div(c, levels), lax.rem(c, levels)]
                    bm = b * m
                    dm = d * m
                    side = side_of(pair, g)
                    from_s = jnp.where(first_lane, side, roll_lanes(dm - bm, 1))
                    from_n = jnp.where(last_lane, side, back(dm + bm, 1))
                    value = lam[c, rows, :] + VERTICAL_MIX * vert - 4.0 * dm + from_s + from_n
                    value = value + d * (m_w + m_e) + (a_e * m_e - a_w * m_w)
                    if (g + 1) * each <= levels:
                        value = value + push
                    elif g * each < levels:
                        value = value + jnp.where(c < levels, 1.0, 0.0) * push
                    if last:
                        out_ref[c] = value
                    else:
                        lam[c, rows, :] = value
                if last:
                    continue
                m, m_e, m_w = smu[s + 1, rows, :], smu[s + 1, rows_e, :], smu[s + 1, rows_w, :]
                bm = bf[step, 1, rows, :] * m
                dm = sdiff[s] * m
                value = slam[s, rows, :] + VERTICAL_MIX * strip_vertical(smu, s, rows, m) - 4.0 * dm
                value = value + roll_lanes(dm - bm, 1) + back(dm + bm, 1) + sdiff[s] * (m_w + m_e)
                value = value + (af[step, 1, rows_e, :] * m_e - af[step, 1, rows_w, :] * m_w)
                slam[s, rows, :] = value + jnp.where(channel_of(s) < levels, prow[1, rows, :], 0.0)
            return carry

        over(body)

    for step in reversed(range(ITERS)):
        if step == ITERS - 1:
            over(weigh)
        else:
            sums(step)
        wrap_strips(smu)
        results = []
        for g in blocks:
            rows = slice(g, g + SUB)
            parts = []
            for k in range(2):
                value = lh[k, rows, :]
                prow[k, rows, :] = (BUOYANCY / levels) * wf[k, rows, :] * value
                turn = (0.25 * ADVECTION) * gu[k, rows, :]
                spread = HEIGHT_DIFFUSION * value
                damp = jnp.tanh(hf[step, k, rows, :])
                kept = value - 4.0 * spread - HEIGHT_DAMPING * (1.0 - damp * damp) * value
                before, after = slice(g - 1, g - 1 + SUB), slice(g + 1, g + 1 + SUB)
                kept = kept + HEIGHT_DIFFUSION * (lh[k, before, :] + lh[k, after, :])
                kept = kept + (0.25 * ADVECTION) * (gv[k, after, :] - gv[k, before, :])
                parts.append((kept, spread + turn, spread - turn))
            (main, to_n, to_s), (piece, piece_n, piece_s) = parts
            side = side_of(edges(piece_n, piece_s), 0)
            main = main + jnp.where(first_lane, side, roll_lanes(to_n, 1)) + jnp.where(last_lane, side, back(to_s, 1))
            piece = piece + roll_lanes(piece_n, 1) + back(piece_s, 1)
            results.append((main, jnp.where(inside, piece, 0.0)))
        for g, result in zip(blocks, results):
            for k in range(2):
                lh[k, g:g + SUB, :] = result[k]
        adjoint(step)

    outh_ref[...] = lh[0, own, :]


def local(checkpoint, holder_list, height, land_mask, diffusivity, tracer_weight, height_weight):
    n, n_y = lax.axis_size("gx"), lax.axis_size("gy")
    width_x, width_y = height.shape
    assert (width_x, width_y) == (SUB, LANE)
    levels = diffusivity.shape[1]
    channels = 3 * levels
    each = channels // GROUPS
    piece_rows = checkpoint.shape[3] // LANE
    padded = -(-piece_rows // SUB) * SUB
    f32 = jnp.float32
    vmem = pl.BlockSpec(memory_space=pltpu.VMEM)
    tile = pltpu.VMEM((SUB, LANE), f32)
    field = pltpu.VMEM((2, 3 * SUB, LANE), f32)
    fields = pltpu.VMEM((ITERS, 2, 3 * SUB, LANE), f32)
    volume = pltpu.VMEM((channels, 3 * SUB, LANE), f32)

    def strips(*lead):
        return pltpu.VMEM((*lead, 3 * SUB, LANE), f32)

    half = channels * HALO // SUB
    out, out_h = pl.pallas_call(
        functools.partial(kernel, n, n_y, levels, piece_rows),
        out_shape=(
            jax.ShapeDtypeStruct((channels, SUB, LANE), f32),
            jax.ShapeDtypeStruct((SUB, LANE), f32),
        ),
        in_specs=[pl.BlockSpec(memory_space=pltpu.HBM)] * 7,
        out_specs=(vmem, vmem),
        scratch_shapes=[
            pltpu.VMEM((n * padded, LANE), f32),
            pltpu.VMEM((n, padded, LANE), f32),
            pltpu.VMEM((ITERS, channels, 3 * SUB, LANE), f32),
            strips(ITERS, each + 2),
            volume, strips(each),
            volume, strips(each + 2),
            pltpu.VMEM((3, channels, 3 * SUB, LANE), f32), strips(3, each),
            strips(each),
            pltpu.VMEM((each, SUB, LANE), f32),
            fields, fields, fields,
            field, field, field, field, field,
            strips(8),
            pltpu.VMEM((8, SUB, LANE), f32),
            strips(2, 8),
            pltpu.VMEM((3, each // 2, SUB, LANE), f32),
            strips(3, 2, each // 2),
            pltpu.VMEM((2, 2, half, SUB, LANE), f32),
            pltpu.VMEM((2, 2, half, SUB, LANE), f32),
            pltpu.VMEM((2, half // 2, SUB, LANE), f32),
            pltpu.VMEM((2, half // 2, SUB, LANE), f32),
            pltpu.SMEM(holder_list.shape, jnp.int32),
            pltpu.SMEM(diffusivity.shape, f32),
            pltpu.VMEM(checkpoint.shape[2:], f32),
            tile,
            pltpu.VMEM((SUB, LANE), jnp.int32),
            tile,
            pltpu.SemaphoreType.DMA((n,)),
            pltpu.SemaphoreType.DMA((n,)),
            pltpu.SemaphoreType.DMA((48,)),
            pltpu.SemaphoreType.DMA((48,)),
            pltpu.SemaphoreType.DMA((7,)),
        ],
        compiler_params=pltpu.CompilerParams(
            collective_id=0, has_side_effects=True, vmem_limit_bytes=60 * 2**20
        ),
    )(
        holder_list, diffusivity, checkpoint.reshape(checkpoint.shape[2:]), height, land_mask,
        tracer_weight.reshape(channels, SUB, LANE), height_weight,
    )
    return out.reshape(tracer_weight.shape), out_h


def solution(mesh):
    return jax.shard_map(
        local,
        mesh=mesh,
        in_specs=(
            P(("member", "gx"), "gy", None, None),
            P(("member", "gx"), "gy", None),
            P(("member", "gx"), "gy"),
            P("gx", "gy"),
            P(),
            P("member", None, "gx", "gy"),
            P(("member", "gx"), "gy"),
        ),
        out_specs=(P("member", None, "gx", "gy"), P(("member", "gx"), "gy")),
        check_vma=False,
    )
```

profile of v0, /device:TPU:0, one launch (start us, length us, event | category | flops | bytes accessed | tf_op | source)
XLA Modules:
  0.0 40.8 jit_solution(6272791016641360438)
XLA Ops:
  0.6 38.0 %shard_map.86 = (f32[48,8,128]{2,1,0:T(8,128)}, f32[8,128]{1,0:T(8,128)}) custom-call(s32[1,1,4]{2,1,0:T(1,128)} %holder_hbm.1, f32[3,16]{1,0:T(4,128)} %diff_hbm.1, f32[4,12288]{1,0:T(4,128)} %bitcast.3, f32[8,128]{1,0:T(8,128)} %height_hbm.1, s32[8,128]{1,0:T(8,128)} %mask_hbm.1, f32[48,8,128]{2,1,0:T(8,128)} %bitcast.4, f32[8,128]{1,0:T(8,128)} %hw_hbm.1), custom_call_target="tpu_custom_call" | custom-call | tf_op jit(solution)/shard_map/pallas_call | solution.py:610
  38.6 0.0 copy-start
  38.6 1.6 %copy.11 = f32[3,16,8,128]{3,2,1,0:T(8,128)} copy(f32[3,16,8,128]{3,2,1,0:T(8,128)} %bitcast.5) | data formatting | bytes 393216
  40.2 0.0 copy-done
  40.3 0.6 %copy.12 = f32[8,128]{1,0:T(8,128)} copy(f32[8,128]{1,0:T(8,128)S(1)} %copy-done) | data formatting | bytes 8192
Async XLA Ops:
  38.6 1.6 %copy-start = (f32[8,128]{1,0:T(8,128)S(1)}, f32[8,128]{1,0:T(8,128)}, u32[]{:S(2)}) copy-start(f32[8,128]{1,0:T(8,128)} %get-tuple-element.9) | copy-start | bytes 12292
where the time goes:
time: 41 us; the launch traced here: 40.8 us
  Pallas kernels  38 us (93%)
  local copies, waits for them, and re-layouts  2.21 us (5%)
  between operations  0.65 us (2%)
    pallas_call x1, Pallas kernels, local(): pl.pallas_call(functools.partial(kernel, n, n_y, levels, piece_rows), out...  38 us
    unnamed x4, local copies, waits for them, and re-layouts  2.21 us

commit v1 on v0

--- a/solution.py
+++ b/solution.py
@@ -144,13 +144,15 @@
         return (channel_of(s) & (levels - 1)) == levels - 1
 
     def level_up(c):
-        return c - lax.div(lax.rem(c, levels) + (levels - 1), levels)
+        return c - 1 if c % levels else c
 
     def level_down(c):
-        return c + lax.div(2 * (levels - 1) - lax.rem(c, levels), levels)
+        return c + 1 if (c + 1) % levels else c
 
     def over(body, carry=0):
-        return lax.fori_loop(0, each, body, carry, unroll=2)
+        for s in range(each):
+            carry = body(s, carry)
+        return carry
 
     def pack_field(value):
         south_part = (lane >= HALO) & (lane < 2 * HALO)
@@ -377,7 +379,7 @@
                     if step < 2:
                         dy[step, c, rows, :] = delta
                     lap = c_e + c_w + c_n + c_s - 4.0 * value
-                    d = diff_ref[lax.div(c, levels), lax.rem(c, levels)]
+                    d = diff_ref[c // levels, c % levels]
                     state[step + 1, c, rows, :] = value + w * (
                         d * lap - a * (c_e - c_w) - b * delta + VERTICAL_MIX * vert
                     )
@@ -524,7 +526,7 @@
                     m = mu[c, rows, :]
                     m_e, m_w = mu[c, rows_e, :], mu[c, rows_w, :]
                     vert = mu[level_up(c), rows, :] + mu[level_down(c), rows, :] - 2.0 * m
-                    d = diff_ref[lax.div(c, levels), lax.rem(c, levels)]
+                    d = diff_ref[c // levels, c % levels]
                     bm = b * m
                     dm = d * m
                     side = side_of(pair, g)
@@ -532,10 +534,8 @@
                     from_n = jnp.where(last_lane, side, back(dm + bm, 1))
                     value = lam[c, rows, :] + VERTICAL_MIX * vert - 4.0 * dm + from_s + from_n
                     value = value + d * (m_w + m_e) + (a_e * m_e - a_w * m_w)
-                    if (g + 1) * each <= levels:
+                    if c < levels:
                         value = value + push
-                    elif g * each < levels:
-                        value = value + jnp.where(c < levels, 1.0, 0.0) * push
                     if last:
                         out_ref[c] = value
                     else:
@@ -609,10 +609,7 @@
     half = channels * HALO // SUB
     out, out_h = pl.pallas_call(
         functools.partial(kernel, n, n_y, levels, piece_rows),
-        out_shape=(
-            jax.ShapeDtypeStruct((channels, SUB, LANE), f32),
-            jax.ShapeDtypeStruct((SUB, LANE), f32),
-        ),
+        out_shape=(pltpu.VMEM((channels, SUB, LANE), f32), pltpu.VMEM((SUB, LANE), f32)),
         in_specs=[pl.BlockSpec(memory_space=pltpu.HBM)] * 7,
         out_specs=(vmem, vmem),
         scratch_shapes=[

time: 41 us -> 37.2 us (0.907)
  Pallas kernels: 38 us -> 35.1 us
  local copies, waits for them, and re-layouts: 2.21 us -> 1.27 us
    pallas_call x1, Pallas kernels: 38 us -> 35.1 us  [local(): pl.pallas_call(functools.partial(kernel, n, n_y, levels, piece_rows), out...]
    unnamed x4 -> x2, local copies, waits for them, and re-layouts: 2.21 us -> 1.27 us
where the time goes in v1:
time: 37.2 us; the launch traced here: 37.1 us
  Pallas kernels  35.1 us (94%)
  local copies, waits for them, and re-layouts  1.27 us (3%)
  between operations  0.64 us (2%)
    pallas_call x1, Pallas kernels, local(): pl.pallas_call(functools.partial(kernel, n, n_y, levels, piece_rows), out...  35.1 us
    unnamed x2, local copies, waits for them, and re-layouts  1.27 us

profile of v1, /device:TPU:0, one launch (start us, length us, event | category | flops | bytes accessed | tf_op | source)
XLA Modules:
  0.0 37.1 jit_solution(7923531091177735355)
XLA Ops:
  0.6 35.1 %shard_map.86 = (f32[48,8,128]{2,1,0:T(8,128)S(1)}, f32[8,128]{1,0:T(8,128)S(1)}) custom-call(s32[1,1,4]{2,1,0:T(1,128)} %holder_hbm.1, f32[3,16]{1,0:T(4,128)} %diff_hbm.1, f32[4,12288]{1,0:T(4,128)} %bitcast.4, f32[8,128]{1,0:T(8,128)} %height_hbm.1, s32[8,128]{1,0:T(8,128)} %mask_hbm.1, f32[48,8,128]{2,1,0:T(8,128)} %bitcast.5, f32[8,128]{1,0:T(8,128)} %hw_hbm.1), custom_call_target="tpu_custom_call" | custom-call | tf_op jit(solution)/shard_map/pallas_call | solution.py:610
  35.8 0.7 %copy.11 = f32[3,16,8,128]{3,2,1,0:T(8,128)} copy(f32[3,16,8,128]{3,2,1,0:T(8,128)S(1)} %bitcast.3) | data formatting | bytes 393216
  36.5 0.6 %copy.12 = f32[8,128]{1,0:T(8,128)} copy(f32[8,128]{1,0:T(8,128)S(1)} %get-tuple-element.7) | data formatting | bytes 8192

commit v2 on v1

--- a/solution.py
+++ b/solution.py
@@ -160,44 +160,63 @@
         picked = jnp.where(south_part, roll_lanes(value, HALO), jnp.where(north_part, roll_lanes(value, 3 * HALO), 0.0))
         return everywhere(picked)
 
+    outer = (slice(0, SUB), slice(2 * SUB, 3 * SUB))
+
+    def both(ref):
+        return jnp.where(sub < HALO, ref[outer[1], :], ref[outer[0], :])
+
+    def fetch(ref, rows):
+        return both(ref) if rows is outer else ref[rows, :]
+
+    def place_at(ref, rows, value):
+        for part in rows if rows is outer else (rows,):
+            ref[part, :] = value
+
     def pack_strip(ref, s, rows):
         packed = zero
         for g in range(GROUPS):
-            moved = roll_lanes(ref[g * each + s, rows, :], (g * GROUP + 2 * HALO) % LANE)
+            moved = roll_lanes(fetch(ref.at[g * each + s], rows), (g * GROUP + 2 * HALO) % LANE)
             packed = jnp.where(group == g, moved, packed)
         return packed
 
-    def send_strips(which, ref):
+    lower_half, upper_half = pl.ds(0, HALO), pl.ds(HALO, HALO)
+    before, after = pl.ds(HALO, HALO), pl.ds(4 * HALO, HALO)
+
+    def send_strips(which, ref, hold=None):
         def body(q, carry):
             a, b = pack_strip(ref, 2 * q, own), pack_strip(ref, 2 * q + 1, own)
+            if hold is not None:
+                hold[2 * q + 1, own, :], hold[2 * q + 2, own, :] = a, b
             zq[which, q] = jnp.where(half, back(a, HALO), roll_lanes(b, HALO))
             return carry
 
         lax.fori_loop(0, each // 2, body, 0, unroll=True)
-        whole = zq.at[which]
         copies = []
         for side, other in enumerate((north, south)):
-            for start, device in (
-                (SUB, {"gy": other}), (0, {"gx": east, "gy": other}), (2 * SUB, {"gx": west, "gy": other}),
+            for source, target, device in (
+                (pl.ds(0, SUB), pl.ds(SUB, SUB), {"gy": other}),
+                (upper_half, before, {"gx": east, "gy": other}),
+                (lower_half, after, {"gx": west, "gy": other}),
             ):
-                copies.append(send(whole, zl.at[which, side, :, pl.ds(start, SUB)], device))
+                copies.append(send(zq.at[which, :, source], zl.at[which, side, :, target], device))
         return copies
 
+    def merge(which, s, rows, packed):
+        q, odd = s // 2, s % 2
+        from_south, from_north = fetch(zl.at[which, 0, q], rows), fetch(zl.at[which, 1, q], rows)
+        if odd:
+            from_south = back(from_south, GROUP // 2)
+        else:
+            from_north = roll_lanes(from_north, GROUP // 2)
+        mid = jnp.where(half, back(packed, HALO), roll_lanes(packed, HALO))
+        value = jnp.where(low, from_south, jnp.where(high, from_north, mid))
+        return jnp.where(inside, value, 0.0)
+
     def build_strips(which, ref, put):
-        def body(q, carry):
+        for s in range(each):
             for g in blocks:
                 rows = slice(g, g + SUB)
-                south_pair, north_pair = zl[which, 0, q, rows, :], zl[which, 1, q, rows, :]
-                for k, (from_south, from_north) in enumerate((
-                    (south_pair, roll_lanes(north_pair, GROUP // 2)), (back(south_pair, GROUP // 2), north_pair),
-                )):
-                    packed = pack_strip(ref, 2 * q + k, rows)
-                    mid = jnp.where(half, back(packed, HALO), roll_lanes(packed, HALO))
-                    value = jnp.where(low, from_south, jnp.where(high, from_north, mid))
-                    put(2 * q + k, rows, jnp.where(inside, value, 0.0))
-            return carry
-
-        lax.fori_loop(0, each // 2, body, 0)
+                put(s, rows, merge(which, s, rows, pack_strip(ref, s, rows)))
 
     def send_rows(ref, out, into, width, to_east, to_west):
         count = channels * width // SUB
@@ -230,20 +249,25 @@
 
         lax.fori_loop(0, count, body, 0, unroll=4)
 
+    def send_direct(ref):
+        return [
+            send(ref.at[:, pl.ds(3 * HALO, HALO)], ref.at[:, pl.ds(HALO, HALO)], {"gx": east}),
+            send(ref.at[:, pl.ds(2 * HALO, HALO)], ref.at[:, pl.ds(4 * HALO, HALO)], {"gx": west}),
+        ]
+
     def send_fields(first, values):
         for k, value in enumerate(values):
             em[first + k, own, :] = value
             es[first + k] = pack_field(value)
         which = pl.ds(first, len(values))
-        mid, before, after = pl.ds(SUB, SUB), pl.ds(0, SUB), pl.ds(2 * SUB, SUB)
         copies = [
-            send(em.at[which, mid], em.at[which, before], {"gx": east}),
-            send(em.at[which, mid], em.at[which, after], {"gx": west}),
+            send(em.at[which, pl.ds(3 * HALO, HALO)], em.at[which, before], {"gx": east}),
+            send(em.at[which, pl.ds(2 * HALO, HALO)], em.at[which, after], {"gx": west}),
         ]
         for side, other in enumerate((north, south)):
-            copies.append(send(es.at[which], el.at[side, which, mid], {"gy": other}))
-            copies.append(send(es.at[which], el.at[side, which, before], {"gx": east, "gy": other}))
-            copies.append(send(es.at[which], el.at[side, which, after], {"gx": west, "gy": other}))
+            copies.append(send(es.at[which], el.at[side, which, pl.ds(SUB, SUB)], {"gy": other}))
+            copies.append(send(es.at[which, upper_half], el.at[side, which, before], {"gx": east, "gy": other}))
+            copies.append(send(es.at[which, lower_half], el.at[side, which, after], {"gx": west, "gy": other}))
         return copies
 
     def take_field(k, target):
@@ -342,9 +366,9 @@
                 at = SUB + row % SUB
                 first[row // SUB, at:at + 1, :] = recv[holder, r:r + 1, :]
 
-    start_copies = send_rows(first, xs.at[0], xr.at[0], HALO, 3 * HALO, 2 * HALO)
-    start_copies += send_strips(0, first)
-    weight_copies = send_rows(lam, xs.at[1], xr.at[1], HALO, 3 * HALO, 2 * HALO)
+    start_copies = send_direct(first)
+    edge_copies = send_strips(0, first, strip.at[0])
+    weight_copies = send_direct(lam)
     weight_copies += send_strips(1, lam)
 
     wait_all(fields_a)
@@ -353,57 +377,78 @@
     take_field(2, lh)
 
     def put_first(s, rows, value):
-        strip[0, s + 1, rows, :] = value
-        pairs[s, rows, :] = edges(value, value)
-
+        place_at(strip.at[0, s + 1], rows, value)
+        place_at(pairs.at[s], rows, edges(value, value))
+
+    def roll_pass(step, s, rows):
+        pair = fetch(pairs.at[s], rows)
+        for g in range(GROUPS):
+            c = g * each + s
+            value = fetch(state.at[step, c], rows)
+            side = side_of(pair, g)
+            c_s = jnp.where(first_lane, side, roll_lanes(value, 1))
+            c_n = jnp.where(last_lane, side, back(value, 1))
+            place_at(dy.at[step, c], rows, c_n - c_s)
+            place_at(mu.at[c], rows, c_n + c_s)
+        value = fetch(strip.at[step, s + 1], rows)
+        c_s, c_n = roll_lanes(value, 1), back(value, 1)
+        place_at(sdy.at[step, s], rows, c_n - c_s)
+        place_at(smu.at[s], rows, c_n + c_s)
+
+    def inner_rolls(s, carry):
+        roll_pass(0, s, own)
+        return carry
+
+    def outer_rolls(s, carry):
+        roll_pass(0, s, outer)
+        return carry
+
+    wait_all(edge_copies[0::3])
+    for s in range(each):
+        put_first(s, own, merge(0, s, own, strip[0, s + 1, own, :]))
+    lax.fori_loop(0, each, inner_rolls, 0, unroll=3)
+    wait_all(edge_copies[1::3] + edge_copies[2::3])
     wait_all(start_copies)
-    take_rows(first, xr.at[0], HALO, HALO, 2 * SUB)
-    build_strips(0, first, put_first)
+    for s in range(each):
+        put_first(s, outer, merge(0, s, outer, pack_strip(first, s, outer)))
+    lax.fori_loop(0, each, outer_rolls, 0, unroll=3)
     wrap_strips(strip.at[0])
 
     def forward(step):
-        def body(s, carry):
+        def roll_body(s, carry):
+            for r in blocks:
+                roll_pass(step, s, slice(r, r + SUB))
+            return carry
+
+        if step:
+            lax.fori_loop(0, each, roll_body, 0, unroll=3)
+        for s in range(each):
             for r in blocks:
                 rows, rows_e, rows_w = (slice(r + d, r + d + SUB) for d in (0, 1, -1))
-                pair = pairs[s, rows, :]
                 a, b, w = af[step, 0, rows, :], bf[step, 0, rows, :], wf[0, rows, :]
                 for g in range(GROUPS):
                     c = g * each + s
                     value = state[step, c, rows, :]
-                    side = side_of(pair, g)
-                    c_s = jnp.where(first_lane, side, roll_lanes(value, 1))
-                    c_n = jnp.where(last_lane, side, back(value, 1))
                     c_e, c_w = state[step, c, rows_e, :], state[step, c, rows_w, :]
-                    vert = state[step, level_up(c), rows, :] + state[step, level_down(c), rows, :] - 2.0 * value
-                    delta = c_n - c_s
-                    if step < 2:
-                        dy[step, c, rows, :] = delta
-                    lap = c_e + c_w + c_n + c_s - 4.0 * value
+                    levels_sum = state[step, level_up(c), rows, :] + state[step, level_down(c), rows, :]
                     d = diff_ref[c // levels, c % levels]
-                    state[step + 1, c, rows, :] = value + w * (
-                        d * lap - a * (c_e - c_w) - b * delta + VERTICAL_MIX * vert
-                    )
+                    change = d * (c_e + c_w + mu[c, rows, :]) + VERTICAL_MIX * levels_sum
+                    change = change - (4.0 * d + 2.0 * VERTICAL_MIX) * value
+                    state[step + 1, c, rows, :] = value + w * (change - a * (c_e - c_w) - b * dy[step, c, rows, :])
                 a, b, w = af[step, 1, rows, :], bf[step, 1, rows, :], wf[1, rows, :]
                 value = strip[step, s + 1, rows, :]
-                c_s, c_n = roll_lanes(value, 1), back(value, 1)
                 c_e, c_w = strip[step, s + 1, rows_e, :], strip[step, s + 1, rows_w, :]
-                delta = c_n - c_s
-                if step < 2:
-                    sdy[step, s, rows, :] = delta
-                lap = c_e + c_w + c_n + c_s - 4.0 * value
+                lap = c_e + c_w + smu[s, rows, :] - 4.0 * value
                 vert = strip_vertical(strip.at[step], s, rows, value)
-                value = value + w * (sdiff[s] * lap - a * (c_e - c_w) - b * delta + VERTICAL_MIX * vert)
+                value = value + w * (sdiff[s] * lap - a * (c_e - c_w) - b * sdy[step, s, rows, :] + VERTICAL_MIX * vert)
                 strip[step + 1, s + 1, rows, :] = value
                 pairs[s, rows, :] = edges(value, value)
-            return carry
-
-        over(body)
 
     outer_copies, fields_b = [], []
     for step in range(ITERS - 1):
         slopes(step, True)
         if step == 1:
-            fields_b = send_fields(3, (hf[2, 0, own, :],))
+            pass
         forward(step)
         if step == 1:
             outer_copies = send_rows(state.at[2], ys, yr, 2, 3 * HALO, 2 * HALO + 2)
@@ -426,13 +471,12 @@
         return total_u, total_v
 
     total_u, total_v = over(last_sums, (zero, zero))
-    fields_c = send_fields(4, (total_u, total_v, hf[3, 0, own, :], af[3, 0, own, :]))
+    fields_c = send_fields(3, (hf[2, 0, own, :], total_u, total_v, hf[3, 0, own, :]))
 
     def put_weight(s, rows, value):
         slam[s, rows, :] = value
 
     wait_all(weight_copies)
-    take_rows(lam, xr.at[1], HALO, HALO, 2 * SUB)
     build_strips(1, lam, put_weight)
 
     def spread_pair(step, s, rows, m):
@@ -463,28 +507,26 @@
         return carry
 
     over(outer_slopes)
-    wait_all(fields_b)
-    take_field(3, hf.at[2])
-    slopes(2, False)
-    wait_all(fields_c)
-    take_field(4, gu)
-    take_field(5, gv)
-    take_field(6, hf.at[3])
-    slopes(3, False)
-    take_field(7, af.at[3])
-    for copy in a2a + sends:
-        copy.wait_send()
-
     def weigh(s, carry):
         for r in blocks:
             rows = slice(r, r + SUB)
             for g in range(GROUPS):
                 c = g * each + s
                 mu[c, rows, :] = wf[0, rows, :] * lam[c, rows, :]
-            m = wf[1, rows, :] * slam[s, rows, :]
-            smu[s + 1, rows, :] = m
-            spread_pair(3, s, rows, m)
+            smu[s + 1, rows, :] = wf[1, rows, :] * slam[s, rows, :]
         return carry
+
+    over(weigh)
+    wrap_strips(smu)
+    wait_all(fields_c)
+    take_field(3, hf.at[2])
+    slopes(2, False)
+    take_field(4, gu)
+    take_field(5, gv)
+    take_field(6, hf.at[3])
+    slopes(3, False)
+    for copy in a2a + sends:
+        copy.wait_send()
 
     def sums(step):
         def body(s, carry):
@@ -555,10 +597,13 @@
 
     for step in reversed(range(ITERS)):
         if step == ITERS - 1:
-            over(weigh)
+            for s in range(each):
+                for r in blocks:
+                    rows = slice(r, r + SUB)
+                    spread_pair(3, s, rows, smu[s + 1, rows, :])
         else:
             sums(step)
-        wrap_strips(smu)
+            wrap_strips(smu)
         results = []
         for g in blocks:
             rows = slice(g, g + SUB)

time: 37.2 us -> 34.2 us (0.919); the launches traced: 37.1 us -> 33.7 us
  Pallas kernels: 35.1 us -> 31.8 us
    pallas_call x1, Pallas kernels: 35.1 us -> 31.8 us  [local(): pl.pallas_call(functools.partial(kernel, n, n_y, levels, piece_rows), out...]
where the time goes in v2:
time: 34.2 us; the launch traced here: 33.7 us
  Pallas kernels  31.8 us (93%)
  local copies, waits for them, and re-layouts  1.27 us (4%)
  between operations  0.64 us (2%)
    pallas_call x1, Pallas kernels, local(): pl.pallas_call(functools.partial(kernel, n, n_y, levels, piece_rows), out...  31.8 us
    unnamed x2, local copies, waits for them, and re-layouts  1.27 us

profile of v2, /device:TPU:0, one launch (start us, length us, event | category | flops | bytes accessed | tf_op | source)
XLA Modules:
  0.0 33.7 jit_solution(16941260048174940711)
XLA Ops:
  0.6 31.8 %shard_map.86 = (f32[48,8,128]{2,1,0:T(8,128)S(1)}, f32[8,128]{1,0:T(8,128)S(1)}) custom-call(s32[1,1,4]{2,1,0:T(1,128)} %holder_hbm.1, f32[3,16]{1,0:T(4,128)} %diff_hbm.1, f32[4,12288]{1,0:T(4,128)} %bitcast.4, f32[8,128]{1,0:T(8,128)} %height_hbm.1, s32[8,128]{1,0:T(8,128)} %mask_hbm.1, f32[48,8,128]{2,1,0:T(8,128)} %bitcast.5, f32[8,128]{1,0:T(8,128)} %hw_hbm.1), custom_call_target="tpu_custom_call" | custom-call | tf_op jit(solution)/shard_map/pallas_call | solution.py:655
  32.4 0.7 %copy.11 = f32[3,16,8,128]{3,2,1,0:T(8,128)} copy(f32[3,16,8,128]{3,2,1,0:T(8,128)S(1)} %bitcast.3) | data formatting | bytes 393216
  33.1 0.6 %copy.12 = f32[8,128]{1,0:T(8,128)} copy(f32[8,128]{1,0:T(8,128)S(1)} %get-tuple-element.7) | data formatting | bytes 8192

commit v3 on v2

--- a/solution.py
+++ b/solution.py
@@ -351,6 +351,7 @@
             gu[k, r:r + SUB, :] = zero
             gv[k, r:r + SUB, :] = zero
 
+    weight_edges = send_strips(1, lam)
     for copy in a2a:
         copy.wait_recv()
     first = state.at[0]
@@ -368,8 +369,7 @@
 
     start_copies = send_direct(first)
     edge_copies = send_strips(0, first, strip.at[0])
-    weight_copies = send_direct(lam)
-    weight_copies += send_strips(1, lam)
+    weight_copies = send_direct(lam) + weight_edges
 
     wait_all(fields_a)
     take_field(0, hf.at[0])

time: 34.2 us -> 33.8 us (0.988); the launches traced: 33.7 us -> 33.6 us
  no operation moved by 1% of the time
where the time goes in v3:
time: 33.8 us; the launch traced here: 33.6 us
  Pallas kernels  31.7 us (94%)
  local copies, waits for them, and re-layouts  1.27 us (4%)
  between operations  0.64 us (2%)
    pallas_call x1, Pallas kernels, local(): pl.pallas_call(functools.partial(kernel, n, n_y, levels, piece_rows), out...  31.7 us
    unnamed x2, local copies, waits for them, and re-layouts  1.27 us

profile of v3, /device:TPU:0, one launch (start us, length us, event | category | flops | bytes accessed | tf_op | source)
XLA Modules:
  0.0 33.6 jit_solution(17327420645311178193)
XLA Ops:
  0.6 31.7 %shard_map.86 = (f32[48,8,128]{2,1,0:T(8,128)S(1)}, f32[8,128]{1,0:T(8,128)S(1)}) custom-call(s32[1,1,4]{2,1,0:T(1,128)} %holder_hbm.1, f32[3,16]{1,0:T(4,128)} %diff_hbm.1, f32[4,12288]{1,0:T(4,128)} %bitcast.4, f32[8,128]{1,0:T(8,128)} %height_hbm.1, s32[8,128]{1,0:T(8,128)} %mask_hbm.1, f32[48,8,128]{2,1,0:T(8,128)} %bitcast.5, f32[8,128]{1,0:T(8,128)} %hw_hbm.1), custom_call_target="tpu_custom_call" | custom-call | tf_op jit(solution)/shard_map/pallas_call | solution.py:655
  32.4 0.7 %copy.11 = f32[3,16,8,128]{3,2,1,0:T(8,128)} copy(f32[3,16,8,128]{3,2,1,0:T(8,128)S(1)} %bitcast.3) | data formatting | bytes 393216
  33.1 0.6 %copy.12 = f32[8,128]{1,0:T(8,128)} copy(f32[8,128]{1,0:T(8,128)S(1)} %get-tuple-element.7) | data formatting | bytes 8192

commit v4 on v3

--- a/solution.py
+++ b/solution.py
@@ -451,8 +451,8 @@
             pass
         forward(step)
         if step == 1:
-            outer_copies = send_rows(state.at[2], ys, yr, 2, 3 * HALO, 2 * HALO + 2)
-            outer_copies += send_strips(2, state.at[2])
+            outer_edges = send_strips(2, state.at[2])
+            outer_copies = send_rows(state.at[2], ys, yr, 2, 3 * HALO, 2 * HALO + 2) + outer_edges
         if step < 2:
             wrap_strips(strip.at[step + 1])
     slopes(3, False)
@@ -593,7 +593,11 @@
                 slam[s, rows, :] = value + jnp.where(channel_of(s) < levels, prow[1, rows, :], 0.0)
             return carry
 
-        over(body)
+        for start in range(0, each, 3):
+            @pl.when(me >= 0)
+            def _(start=start):
+                for s in range(start, start + 3):
+                    body(s, 0)
 
     for step in reversed(range(ITERS)):
         if step == ITERS - 1:

time: 33.8 us -> 33.4 us (0.988)
  Pallas kernels: 31.7 us -> 31.3 us
    pallas_call x1, Pallas kernels: 31.7 us -> 31.3 us  [local(): pl.pallas_call(functools.partial(kernel, n, n_y, levels, piece_rows), out...]
where the time goes in v4:
time: 33.4 us; the launch traced here: 33.3 us
  Pallas kernels  31.3 us (94%)
  local copies, waits for them, and re-layouts  1.27 us (4%)
  between operations  0.64 us (2%)
    pallas_call x1, Pallas kernels, local(): pl.pallas_call(functools.partial(kernel, n, n_y, levels, piece_rows), out...  31.3 us
    unnamed x2, local copies, waits for them, and re-layouts  1.27 us

profile of v4, /device:TPU:0, one launch (start us, length us, event | category | flops | bytes accessed | tf_op | source)
XLA Modules:
  0.0 33.3 jit_solution(5205426350447679241)
XLA Ops:
  0.6 31.3 %shard_map.86 = (f32[48,8,128]{2,1,0:T(8,128)S(1)}, f32[8,128]{1,0:T(8,128)S(1)}) custom-call(s32[1,1,4]{2,1,0:T(1,128)} %holder_hbm.1, f32[3,16]{1,0:T(4,128)} %diff_hbm.1, f32[4,12288]{1,0:T(4,128)} %bitcast.4, f32[8,128]{1,0:T(8,128)} %height_hbm.1, s32[8,128]{1,0:T(8,128)} %mask_hbm.1, f32[48,8,128]{2,1,0:T(8,128)} %bitcast.5, f32[8,128]{1,0:T(8,128)} %hw_hbm.1), custom_call_target="tpu_custom_call" | custom-call | tf_op jit(solution)/shard_map/pallas_call | solution.py:659
  32.0 0.7 %copy.11 = f32[3,16,8,128]{3,2,1,0:T(8,128)} copy(f32[3,16,8,128]{3,2,1,0:T(8,128)S(1)} %bitcast.3) | data formatting | bytes 393216
  32.7 0.6 %copy.12 = f32[8,128]{1,0:T(8,128)} copy(f32[8,128]{1,0:T(8,128)S(1)} %get-tuple-element.7) | data formatting | bytes 8192
